TPU v7x, 256 devices: a whole 4x4x8 slice. The times are simulated.
256 devices in a mesh: dp: 32 (over y, z), cent: 8 (over x, core).
Axes of the slice: x: 4, y: 4, z: 8, core: 2. Of those that a mesh axis runs over, the one named last changes fastest.
Arguments:
- stream: bfloat16 [65536, 768], P('dp'), may hold values from -6 to 6
- sample_index: int32 [32768], P('dp'), may hold values from 0 to 2047
- centroids: float32 [16384, 768], P(('cent', 'dp')), may hold values from -6 to 6
- first_moment: float32 [16384, 768], P(('cent', 'dp')), may hold values from -3 to 3
- second_moment: float32 [16384, 768], P(('cent', 'dp')), may hold values from 0.01 to 1
Outputs:
- new_centroids: float32 [16384, 768], P(('cent', 'dp'))
- new_first: float32 [16384, 768], P(('cent', 'dp'))
- new_second: float32 [16384, 768], P(('cent', 'dp'))
All inputs are finite; a program needn't handle non-finite values.
Results may differ from a plain program's by a relative error of at most 0.0003.
Values may be sent and summed in bfloat16 or wider, within the bound.
A program may use at most 64 MiB of HBM per device.

v0:
```python
import math
import jax
import jax.numpy as jnp
from jax import lax
from jax.sharding import PartitionSpec as P

KB = 16384
ITERS = 3
temper = 2.0
beta_one = 0.9
beta_two = 0.99
step_rate = 0.05
epsilon = 1e-08


def per_device(stream, sample_index, centroids, first_moment, second_moment):
    embedded = stream[sample_index]
    local_rows = embedded.shape[0]
    total_rows = local_rows * lax.axis_size("dp")
    balance = math.log(total_rows / KB)
    rounded = centroids.astype(jnp.bfloat16)
    shard_piece = lax.all_gather(rounded, "dp", axis=0, tiled=True)
    squares = jnp.sum(shard_piece.astype(jnp.float32) ** 2, axis=1)
    product = lax.dot_general(
        embedded, shard_piece, (((1,), (1,)), ((), ())), preferred_element_type=jnp.float32
    )
    logits = (2.0 * product - squares[None, :]) / temper

    def row_potential(column_pot):
        shifted = logits + column_pot[None, :]
        highest = jnp.max(shifted, axis=1)
        summed = jnp.sum(jnp.exp(shifted - highest[:, None]), axis=1)
        overall = lax.pmax(highest, "cent")
        summed = lax.psum(summed * jnp.exp(highest - overall), "cent")
        highest = overall
        return -(highest + jnp.log(summed))

    column_pot = jnp.zeros((logits.shape[1],), jnp.float32)
    for sweep_index in range(ITERS):
        column_shifted = logits + row_potential(column_pot)[:, None]
        column_highest = jnp.max(column_shifted, axis=0)
        column_summed = jnp.sum(jnp.exp(column_shifted - column_highest[None, :]), axis=0)
        column_overall = lax.pmax(column_highest, "dp")
        column_summed = lax.psum(column_summed * jnp.exp(column_highest - column_overall), "dp")
        column_highest = column_overall
        column_pot = balance - (column_highest + jnp.log(column_summed))
    row_pot = row_potential(column_pot)
    transport = jnp.exp(logits + row_pot[:, None] + column_pot[None, :]).astype(jnp.bfloat16)
    weighted = lax.dot_general(
        transport, embedded, (((0,), (0,)), ((), ())), preferred_element_type=jnp.float32
    )
    weight_mass = jnp.sum(transport.astype(jnp.float32), axis=0)
    weighted, weight_mass = lax.psum((weighted, weight_mass), "dp")
    owned_rows = centroids.shape[0]
    offset_rows = lax.axis_index("dp") * owned_rows
    weighted = lax.dynamic_slice_in_dim(weighted, offset_rows, owned_rows, 0)
    weight_mass = lax.dynamic_slice_in_dim(weight_mass, offset_rows, owned_rows, 0)
    gradient = (weight_mass[:, None] * centroids - weighted) * (KB / total_rows)
    new_first = beta_one * first_moment + (1.0 - beta_one) * gradient
    new_second = beta_two * second_moment + (1.0 - beta_two) * gradient * gradient
    new_centroids = centroids - step_rate * new_first / (jnp.sqrt(new_second) + epsilon)
    return (new_centroids, new_first, new_second)


def solution(mesh):
    return jax.shard_map(
        per_device,
        mesh=mesh,
        in_specs=(
            P("dp", None),
            P("dp"),
            P(("cent", "dp"), None),
            P(("cent", "dp"), None),
            P(("cent", "dp"), None),
        ),
        out_specs=(P(("cent", "dp"), None), P(("cent", "dp"), None), P(("cent", "dp"), None)),
        check_vma=False,
    )
```

profile of v0, /device:TPU:1, one launch (start us, length us, event | category | flops | bytes accessed | tf_op | source)
XLA Modules:
  0.0 889.1 jit_solution(12046903474257052355)
XLA Ops:
  9.7 5.2 gather_fusion
  15.0 76.0 %all-gather.2.cloned.1.call-done = bf16[2048,768]{1,0:T(8,128)(2,1)} async-done(((bf16[64,768]{1,0:T(8,128)(2,1)}), bf16[2048,768]{1,0:T(8,128)(2,1)}) %all-gather.2.cloned.1.call-update) | async-done | bytes 3145744 | tf_op jit(solution)/shard_map/all_gather | solution.py:22
  93.6 9.1 %fusion.2 = (f32[1024]{0:T(1024)S(1)}, f32[1024,2048]{1,0:T(8,128)}) fusion(f32[2048]{0:T(1024)S(1)} %multiply_reduce_fusion, bf16[1024,768]{1,0:T(8,128)(2,1)} %gather_fusion, bf16[2048,768]{1,0:T(8,128)(2,1)} %all-gather.2.cloned.1.call-done), kind=kOutput, calls=%fused_computation.39 | convolution fusion | flops 3229613056 | bytes 13119488 | tf_op jit(solution)/shard_map/dot_general | solution.py:24
  102.6 16.4 %pmax.49 = f32[1024]{0:T(1024)S(1)} all-reduce(f32[1024]{0:T(1024)S(1)} %get-tuple-element.6), channel_id=1, replica_groups=mesh['dp'=32,'cent'=8] {'cent'}, use_global_device_ids=true, to_apply=%region_2.0 | all-reduce | flops 1024 | bytes 8192 | tf_op jit(solution)/shard_map/pmax | solution.py:33
  119.0 4.6 exponential_reduce_fusion.6
  123.6 12.4 %psum.63 = f32[1024]{0:T(1024)S(1)} all-reduce(f32[1024]{0:T(1024)S(1)} %exponential_multiply_fusion.6), channel_id=1, replica_groups=mesh['dp'=32,'cent'=8] {'cent'}, use_global_device_ids=true, to_apply=%region_4.0 | all-reduce | flops 1024 | bytes 8192 | tf_op jit(solution)/shard_map/psum | solution.py:34
  140.1 4.3 exponential_reduce_fusion.5
  144.4 58.9 %pmax.50 = f32[2048]{0:T(1024)S(1)} all-reduce(f32[2048]{0:T(1024)S(1)} %add_reduce_fusion.5), channel_id=1, replica_groups=mesh['dp'=32,'cent'=8] {'dp'}, use_global_device_ids=true, to_apply=%region_6.0 | all-reduce | flops 2048 | bytes 16384 | tf_op jit(solution)/shard_map/pmax | solution.py:43
  203.3 56.7 %psum.64 = f32[2048]{0:T(1024)S(1)} all-reduce(f32[2048]{0:T(1024)S(1)} %exponential_multiply_fusion.2), channel_id=1, replica_groups=mesh['dp'=32,'cent'=8] {'dp'}, use_global_device_ids=true, to_apply=%region_8.0 | all-reduce | flops 2048 | bytes 16384 | tf_op jit(solution)/shard_map/psum | solution.py:44
  260.1 4.0 add_reduce_fusion.4
  264.1 4.4 exponential_reduce_fusion.4
  268.5 40.3 %pmax.51 = f32[1024]{0:T(1024)S(1)} all-reduce(f32[1024]{0:T(1024)S(1)} %add_reduce_fusion.4), channel_id=1, replica_groups=mesh['dp'=32,'cent'=8] {'cent'}, use_global_device_ids=true, to_apply=%region_10.0 | all-reduce | flops 1024 | bytes 8192 | tf_op jit(solution)/shard_map/pmax | solution.py:33
  308.8 12.4 %psum.65 = f32[1024]{0:T(1024)S(1)} all-reduce(f32[1024]{0:T(1024)S(1)} %exponential_multiply_fusion.5), channel_id=1, replica_groups=mesh['dp'=32,'cent'=8] {'cent'}, use_global_device_ids=true, to_apply=%region_12.0 | all-reduce | flops 1024 | bytes 8192 | tf_op jit(solution)/shard_map/psum | solution.py:34
  321.2 4.0 add_reduce_fusion.3
  325.3 4.3 exponential_reduce_fusion.3
  329.6 59.1 %pmax.52 = f32[2048]{0:T(1024)S(1)} all-reduce(f32[2048]{0:T(1024)S(1)} %add_reduce_fusion.3), channel_id=1, replica_groups=mesh['dp'=32,'cent'=8] {'dp'}, use_global_device_ids=true, to_apply=%region_14.0 | all-reduce | flops 2048 | bytes 16384 | tf_op jit(solution)/shard_map/pmax | solution.py:43
  388.7 57.2 %psum.66 = f32[2048]{0:T(1024)S(1)} all-reduce(f32[2048]{0:T(1024)S(1)} %exponential_multiply_fusion.1), channel_id=1, replica_groups=mesh['dp'=32,'cent'=8] {'dp'}, use_global_device_ids=true, to_apply=%region_16.0 | all-reduce | flops 2048 | bytes 16384 | tf_op jit(solution)/shard_map/psum | solution.py:44
  446.0 4.0 add_reduce_fusion.2
  450.0 4.4 exponential_reduce_fusion.2
  454.4 39.6 %pmax.53 = f32[1024]{0:T(1024)S(1)} all-reduce(f32[1024]{0:T(1024)S(1)} %add_reduce_fusion.2), channel_id=1, replica_groups=mesh['dp'=32,'cent'=8] {'cent'}, use_global_device_ids=true, to_apply=%region_18.0 | all-reduce | flops 1024 | bytes 8192 | tf_op jit(solution)/shard_map/pmax | solution.py:33
  494.0 12.4 %psum.67 = f32[1024]{0:T(1024)S(1)} all-reduce(f32[1024]{0:T(1024)S(1)} %exponential_multiply_fusion.4), channel_id=1, replica_groups=mesh['dp'=32,'cent'=8] {'cent'}, use_global_device_ids=true, to_apply=%region_20.0 | all-reduce | flops 1024 | bytes 8192 | tf_op jit(solution)/shard_map/psum | solution.py:34
  506.4 4.0 add_reduce_fusion.1
  510.4 4.3 exponential_reduce_fusion.1
  514.7 59.2 %pmax.54 = f32[2048]{0:T(1024)S(1)} all-reduce(f32[2048]{0:T(1024)S(1)} %add_reduce_fusion.1), channel_id=1, replica_groups=mesh['dp'=32,'cent'=8] {'dp'}, use_global_device_ids=true, to_apply=%region_22.0 | all-reduce | flops 2048 | bytes 16384 | tf_op jit(solution)/shard_map/pmax | solution.py:43
  573.9 57.0 %psum.68 = f32[2048]{0:T(1024)S(1)} all-reduce(f32[2048]{0:T(1024)S(1)} %exponential_multiply_fusion), channel_id=1, replica_groups=mesh['dp'=32,'cent'=8] {'dp'}, use_global_device_ids=true, to_apply=%region_24.0 | all-reduce | flops 2048 | bytes 16384 | tf_op jit(solution)/shard_map/psum | solution.py:44
  635.0 4.4 exponential_reduce_fusion
  639.4 39.6 %pmax.55 = f32[1024]{0:T(1024)S(1)} all-reduce(f32[1024]{0:T(1024)S(1)} %add_reduce_fusion), channel_id=1, replica_groups=mesh['dp'=32,'cent'=8] {'cent'}, use_global_device_ids=true, to_apply=%region_26.0 | all-reduce | flops 1024 | bytes 8192 | tf_op jit(solution)/shard_map/pmax | solution.py:33
  679.0 12.4 %psum.69 = f32[1024]{0:T(1024)S(1)} all-reduce(f32[1024]{0:T(1024)S(1)} %exponential_multiply_fusion.3), channel_id=1, replica_groups=mesh['dp'=32,'cent'=8] {'cent'}, use_global_device_ids=true, to_apply=%region_28.0 | all-reduce | flops 1024 | bytes 8192 | tf_op jit(solution)/shard_map/psum | solution.py:34
  692.0 10.4 %fusion.1 = f32[2048,768]{1,0:T(8,128)} fusion(bf16[1024,768]{1,0:T(8,128)(2,1)} %gather_fusion, f32[1024,2048]{1,0:T(8,128)} %get-tuple-element.7, f32[1024]{0:T(1024)S(1)} %add_negate_fusion, f32[2048]{0:T(1024)S(1)} %add_subtract_fusion), kind=kOutput, calls=%fused_computation.38 | convolution fusion | flops 3227516928 | bytes 16265216 | tf_op jit(solution)/shard_map/dot_general | solution.py:49
  702.4 4.3 convert_reduce_fusion
  706.8 61.3 %psum.70 = f32[2048]{0:T(1024)S(1)} all-reduce(f32[2048]{0:T(1024)S(1)} %convert_reduce_fusion), channel_id=1, replica_groups=mesh['dp'=32,'cent'=8] {'dp'}, use_global_device_ids=true, to_apply=%region_30.0 | all-reduce | flops 2048 | bytes 16384 | tf_op jit(solution)/shard_map/psum | solution.py:53
  768.1 112.1 %all-reduce.2.cloned.1.call-done = f32[2048,768]{1,0:T(8,128)} async-done(((f32[2048,768]{1,0:T(8,128)}), f32[2048,768]{1,0:T(8,128)}) %all-reduce.2.cloned.1.call-update) | async-done | bytes 6291472 | tf_op jit(solution)/shard_map/psum | solution.py:53
  (33 shorter events, 15.9 us)
Async XLA Ops:
  7.2 2.6 copy-start
  7.2 83.8 %all-gather.2.cloned.1.call-start = ((), (), s32[]{:S(2)}) async-start(), calls=%async_computation | async-start | bytes 3244032 | tf_op jit(solution)/shard_map/all_gather | solution.py:22
  9.0 871.3 %all-reduce.2.cloned.1.call-start = ((), (), s32[]{:S(2)}) async-start(), calls=%async_computation.1 | async-start | bytes 12582912 | tf_op jit(solution)/shard_map/psum | solution.py:53
  691.4 0.6 copy-start.3
  702.4 177.9 %copy-start.1 = (f32[64,768]{1,0:T(8,128)S(1)}, f32[64,768]{1,0:T(8,128)}, u32[]{:S(2)}) copy-start(f32[64,768]{1,0:T(8,128)} %param.7) | copy-start | bytes 589828
  702.4 177.9 %copy-start.2 = (f32[64,768]{1,0:T(8,128)S(1)}, f32[64,768]{1,0:T(8,128)}, u32[]{:S(2)}) copy-start(f32[64,768]{1,0:T(8,128)} %param.8) | copy-start | bytes 589828
Sparse Core Ops, SparseCore 0:
  11.2 79.7 all-gather.1
  702.5 177.6 all-reduce.1
where the time goes:
time: 890 us; the launch traced here: 889 us
  blocking collectives  595 us (67%)
  waiting for transfers between devices  188 us (21%)
  other arithmetic  66.1 us (7%)
  matrix products  19.4 us (2%)
  between operations  14.3 us (2%)
    pmax x3, blocking collectives, per_device(): column_overall = lax.pmax(column_highest, 'dp')  177 us
    psum x3, blocking collectives, per_device(): lax.psum(column_summed * jnp.exp(column_highest - column_overall), 'dp')  171 us
    pmax x4, blocking collectives, row_potential(): overall = lax.pmax(highest, 'cent')  136 us
    psum x1, waiting for transfers between devices, per_device(): weighted, weight_mass = lax.psum((weighted, weight_mass), 'dp')  112 us
    all_gather x1, waiting for transfers between devices, per_device(): shard_piece = lax.all_gather(rounded, 'dp', axis=0, tiled=True)  76 us
    psum x1, blocking collectives, per_device(): weighted, weight_mass = lax.psum((weighted, weight_mass), 'dp')  61.3 us
    psum x4, blocking collectives, row_potential(): summed = lax.psum(summed * jnp.exp(highest - overall), 'cent')  49.7 us
  transfers between devices with their start and end apart: 2, of which 2 were waited for; matrix products, arithmetic and copies ran while one was open for 1% of the time, Pallas kernels for 0%

commit v1 on v0

--- a/solution.py
+++ b/solution.py
@@ -11,6 +11,10 @@
 beta_two = 0.99
 step_rate = 0.05
 epsilon = 1e-08
+
+
+def column_list(original):
+    return jnp.sum(lax.all_gather(original, "dp"), 0)
 
 
 def per_device(stream, sample_index, centroids, first_moment, second_moment):
@@ -41,7 +45,7 @@
         column_highest = jnp.max(column_shifted, axis=0)
         column_summed = jnp.sum(jnp.exp(column_shifted - column_highest[None, :]), axis=0)
         column_overall = lax.pmax(column_highest, "dp")
-        column_summed = lax.psum(column_summed * jnp.exp(column_highest - column_overall), "dp")
+        column_summed = column_list(column_summed * jnp.exp(column_highest - column_overall))
         column_highest = column_overall
         column_pot = balance - (column_highest + jnp.log(column_summed))
     row_pot = row_potential(column_pot)

time: 890 us -> 828 us (0.930)
  blocking collectives: 595 us -> 527 us
    psum x3 -> x0, blocking collectives: 171 us -> none  [per_device(): lax.psum(column_summed * jnp.exp(column_highest - column_overall), 'dp')]
    all_gather x0 -> x3, blocking collectives: none -> 107 us  [column_list(): return jnp.sum(lax.all_gather(original, 'dp'), 0)]
where the time goes in v1:
time: 828 us; the launch traced here: 827 us
  blocking collectives  527 us (64%)
  waiting for transfers between devices  190 us (23%)
  other arithmetic  68.1 us (8%)
  matrix products  19.4 us (2%)
  between operations  14.2 us (2%)
  local copies, waits for them, and re-layouts  8.42 us (1%)
    pmax x3, blocking collectives, per_device(): column_overall = lax.pmax(column_highest, 'dp')  177 us
    pmax x4, blocking collectives, row_potential(): overall = lax.pmax(highest, 'cent')  131 us
    psum x1, waiting for transfers between devices, per_device(): weighted, weight_mass = lax.psum((weighted, weight_mass), 'dp')  114 us
    all_gather x3, blocking collectives, column_list(): return jnp.sum(lax.all_gather(original, 'dp'), 0)  107 us
    all_gather x1, waiting for transfers between devices, per_device(): shard_piece = lax.all_gather(rounded, 'dp', axis=0, tiled=True)  76 us
    psum x1, blocking collectives, per_device(): weighted, weight_mass = lax.psum((weighted, weight_mass), 'dp')  61.8 us
    psum x4, blocking collectives, row_potential(): summed = lax.psum(summed * jnp.exp(highest - overall), 'cent')  49.7 us
    reduce_sum x4, other arithmetic, row_potential(): summed = jnp.sum(jnp.exp(shifted - highest[:, None]), axis=1)  17.7 us
  transfers between devices with their start and end apart: 2, of which 2 were waited for; matrix products, arithmetic and copies ran while one was open for 1% of the time, Pallas kernels for 0%

profile of v1, /device:TPU:1, one launch (start us, length us, event | category | flops | bytes accessed | tf_op | source)
XLA Modules:
  0.0 827.2 jit_solution(6818301474034213811)
XLA Ops:
  9.7 5.2 gather_fusion
  15.0 76.0 %all-gather.5.cloned.1.call-done = bf16[2048,768]{1,0:T(8,128)(2,1)} async-done(((bf16[64,768]{1,0:T(8,128)(2,1)}), bf16[2048,768]{1,0:T(8,128)(2,1)}) %all-gather.5.cloned.1.call-update) | async-done | bytes 3145744 | tf_op jit(solution)/shard_map/all_gather | solution.py:26
  93.6 9.1 %fusion.2 = (f32[1024]{0:T(1024)S(1)}, f32[1024,2048]{1,0:T(8,128)}) fusion(f32[2048]{0:T(1024)S(1)} %multiply_reduce_fusion, bf16[1024,768]{1,0:T(8,128)(2,1)} %gather_fusion, bf16[2048,768]{1,0:T(8,128)(2,1)} %all-gather.5.cloned.1.call-done), kind=kOutput, calls=%fused_computation.39 | convolution fusion | flops 3229613056 | bytes 13119488 | tf_op jit(solution)/shard_map/dot_general | solution.py:28
  102.6 16.4 %pmax.49 = f32[1024]{0:T(1024)S(1)} all-reduce(f32[1024]{0:T(1024)S(1)} %get-tuple-element.6), channel_id=1, replica_groups=mesh['dp'=32,'cent'=8] {'cent'}, use_global_device_ids=true, to_apply=%region_2.0 | all-reduce | flops 1024 | bytes 8192 | tf_op jit(solution)/shard_map/pmax | solution.py:37
  119.0 4.6 exponential_reduce_fusion.6
  123.6 12.4 %psum.42 = f32[1024]{0:T(1024)S(1)} all-reduce(f32[1024]{0:T(1024)S(1)} %exponential_multiply_fusion.6), channel_id=1, replica_groups=mesh['dp'=32,'cent'=8] {'cent'}, use_global_device_ids=true, to_apply=%region_4.0 | all-reduce | flops 1024 | bytes 8192 | tf_op jit(solution)/shard_map/psum | solution.py:38
  136.1 4.0 add_reduce_fusion.5
  140.1 4.3 exponential_reduce_fusion.5
  144.4 58.9 %pmax.50 = f32[2048]{0:T(1024)S(1)} all-reduce(f32[2048]{0:T(1024)S(1)} %add_reduce_fusion.5), channel_id=1, replica_groups=mesh['dp'=32,'cent'=8] {'dp'}, use_global_device_ids=true, to_apply=%region_6.0 | all-reduce | flops 2048 | bytes 16384 | tf_op jit(solution)/shard_map/pmax | solution.py:47
  203.3 33.9 %all-gather = f32[65536]{0:T(1024)S(1)} all-gather(f32[2048]{0:T(1024)S(1)} %exponential_multiply_fusion.2), channel_id=2, replica_groups=mesh['dp'=32,'cent'=8] {'dp'}, dimensions={0}, use_global_device_ids=true | all-gather | bytes 270336 | tf_op jit(solution)/shard_map/all_gather | solution.py:17
  238.9 4.0 add_reduce_fusion.4
  243.0 4.4 exponential_reduce_fusion.4
  247.3 38.4 %pmax.51 = f32[1024]{0:T(1024)S(1)} all-reduce(f32[1024]{0:T(1024)S(1)} %add_reduce_fusion.4), channel_id=1, replica_groups=mesh['dp'=32,'cent'=8] {'cent'}, use_global_device_ids=true, to_apply=%region_10.0 | all-reduce | flops 1024 | bytes 8192 | tf_op jit(solution)/shard_map/pmax | solution.py:37
  285.7 12.4 %psum.43 = f32[1024]{0:T(1024)S(1)} all-reduce(f32[1024]{0:T(1024)S(1)} %exponential_multiply_fusion.5), channel_id=1, replica_groups=mesh['dp'=32,'cent'=8] {'cent'}, use_global_device_ids=true, to_apply=%region_12.0 | all-reduce | flops 1024 | bytes 8192 | tf_op jit(solution)/shard_map/psum | solution.py:38
  298.2 4.0 add_reduce_fusion.3
  302.2 4.3 exponential_reduce_fusion.3
  306.5 59.1 %pmax.52 = f32[2048]{0:T(1024)S(1)} all-reduce(f32[2048]{0:T(1024)S(1)} %add_reduce_fusion.3), channel_id=1, replica_groups=mesh['dp'=32,'cent'=8] {'dp'}, use_global_device_ids=true, to_apply=%region_14.0 | all-reduce | flops 2048 | bytes 16384 | tf_op jit(solution)/shard_map/pmax | solution.py:47
  365.6 34.3 %all-gather.1 = f32[65536]{0:T(1024)S(1)} all-gather(f32[2048]{0:T(1024)S(1)} %exponential_multiply_fusion.1), channel_id=3, replica_groups=mesh['dp'=32,'cent'=8] {'dp'}, dimensions={0}, use_global_device_ids=true | all-gather | bytes 270336 | tf_op jit(solution)/shard_map/all_gather | solution.py:17
  401.7 4.0 add_reduce_fusion.2
  405.7 4.4 exponential_reduce_fusion.2
  410.1 38.4 %pmax.53 = f32[1024]{0:T(1024)S(1)} all-reduce(f32[1024]{0:T(1024)S(1)} %add_reduce_fusion.2), channel_id=1, replica_groups=mesh['dp'=32,'cent'=8] {'cent'}, use_global_device_ids=true, to_apply=%region_18.0 | all-reduce | flops 1024 | bytes 8192 | tf_op jit(solution)/shard_map/pmax | solution.py:37
  448.4 12.4 %psum.44 = f32[1024]{0:T(1024)S(1)} all-reduce(f32[1024]{0:T(1024)S(1)} %exponential_multiply_fusion.4), channel_id=1, replica_groups=mesh['dp'=32,'cent'=8] {'cent'}, use_global_device_ids=true, to_apply=%region_20.0 | all-reduce | flops 1024 | bytes 8192 | tf_op jit(solution)/shard_map/psum | solution.py:38
  464.9 4.3 exponential_reduce_fusion.1
  469.2 59.1 %pmax.54 = f32[2048]{0:T(1024)S(1)} all-reduce(f32[2048]{0:T(1024)S(1)} %add_reduce_fusion.1), channel_id=1, replica_groups=mesh['dp'=32,'cent'=8] {'dp'}, use_global_device_ids=true, to_apply=%region_22.0 | all-reduce | flops 2048 | bytes 16384 | tf_op jit(solution)/shard_map/pmax | solution.py:47
  528.3 39.2 %all-gather.2 = f32[65536]{0:T(1024)} all-gather(f32[2048]{0:T(1024)S(1)} %exponential_multiply_fusion), channel_id=4, replica_groups=mesh['dp'=32,'cent'=8] {'dp'}, dimensions={0}, use_global_device_ids=true | all-gather | bytes 270336 | tf_op jit(solution)/shard_map/all_gather | solution.py:17
  572.6 4.4 exponential_reduce_fusion
  577.0 38.1 %pmax.55 = f32[1024]{0:T(1024)S(1)} all-reduce(f32[1024]{0:T(1024)S(1)} %add_reduce_fusion), channel_id=1, replica_groups=mesh['dp'=32,'cent'=8] {'cent'}, use_global_device_ids=true, to_apply=%region_26.0 | all-reduce | flops 1024 | bytes 8192 | tf_op jit(solution)/shard_map/pmax | solution.py:37
  615.1 12.4 %psum.45 = f32[1024]{0:T(1024)S(1)} all-reduce(f32[1024]{0:T(1024)S(1)} %exponential_multiply_fusion.3), channel_id=1, replica_groups=mesh['dp'=32,'cent'=8] {'cent'}, use_global_device_ids=true, to_apply=%region_28.0 | all-reduce | flops 1024 | bytes 8192 | tf_op jit(solution)/shard_map/psum | solution.py:38
  628.1 10.4 %fusion.1 = f32[2048,768]{1,0:T(8,128)} fusion(bf16[1024,768]{1,0:T(8,128)(2,1)} %gather_fusion, f32[1024,2048]{1,0:T(8,128)} %get-tuple-element.7, f32[1024]{0:T(1024)S(1)} %add_negate_fusion, f32[2048]{0:T(1024)S(1)} %add_subtract_fusion), kind=kOutput, calls=%fused_computation.38 | convolution fusion | flops 3227516928 | bytes 16265216 | tf_op jit(solution)/shard_map/dot_general | solution.py:53
  638.5 4.3 convert_reduce_fusion
  642.8 61.8 %psum.46 = f32[2048]{0:T(1024)S(1)} all-reduce(f32[2048]{0:T(1024)S(1)} %convert_reduce_fusion), channel_id=1, replica_groups=mesh['dp'=32,'cent'=8] {'dp'}, use_global_device_ids=true, to_apply=%region_30.0 | all-reduce | flops 2048 | bytes 16384 | tf_op jit(solution)/shard_map/psum | solution.py:57
  704.7 113.7 %all-reduce.2.cloned.1.call-done = f32[2048,768]{1,0:T(8,128)} async-done(((f32[2048,768]{1,0:T(8,128)}), f32[2048,768]{1,0:T(8,128)}) %all-reduce.2.cloned.1.call-update) | async-done | bytes 6291472 | tf_op jit(solution)/shard_map/psum | solution.py:57
  (39 shorter events, 20.4 us)
Async XLA Ops:
  7.2 2.6 copy-start
  7.2 83.8 %all-gather.5.cloned.1.call-start = ((), (), s32[]{:S(2)}) async-start(), calls=%async_computation | async-start | bytes 3244032 | tf_op jit(solution)/shard_map/all_gather | solution.py:26
  9.0 809.4 %all-reduce.2.cloned.1.call-start = ((), (), s32[]{:S(2)}) async-start(), calls=%async_computation.1 | async-start | bytes 12582912 | tf_op jit(solution)/shard_map/psum | solution.py:57
  627.5 0.6 copy-start.3
  638.5 179.9 %copy-start.1 = (f32[64,768]{1,0:T(8,128)S(1)}, f32[64,768]{1,0:T(8,128)}, u32[]{:S(2)}) copy-start(f32[64,768]{1,0:T(8,128)} %param.7) | copy-start | bytes 589828
  638.5 179.9 %copy-start.2 = (f32[64,768]{1,0:T(8,128)S(1)}, f32[64,768]{1,0:T(8,128)}, u32[]{:S(2)}) copy-start(f32[64,768]{1,0:T(8,128)} %param.8) | copy-start | bytes 589828
Sparse Core Ops, SparseCore 0:
  11.2 79.7 all-gather.4
  638.6 179.7 all-reduce.1
